TPU v7x, 512 devices: a whole 4x8x8 slice. The times are simulated.
512 devices in a mesh: dp: 128 (over y, z_hi, x), rows: 4 (over z_lo, core).
Axes of the slice: x: 4, y: 8, z: 8 (z_hi: 4, z_lo: 2; z = z_hi * 2 + z_lo), core: 2. Of those that a mesh axis runs over, the one named last changes fastest.
Arguments:
- image_rows: bfloat16 [65536, 1152], P(('dp', 'rows')), may hold values from -1.0234375 to 1.0234375
- text_rows: bfloat16 [65536, 1152], P(('dp', 'rows')), may hold values from -1.0234375 to 1.0234375
- logit_scale: float32 [1], replicated, may hold values from 1 to 3
- logit_bias: float32 [1], replicated, may hold values from -3 to -1
Outputs:
- grad_image: bfloat16 [65536, 1152], P(('dp', 'rows'))
- grad_text: bfloat16 [65536, 1152], P(('dp', 'rows'))
All inputs are finite; a program needn't handle non-finite values.
Results may differ from a plain program's by a relative error of at most 0.015.
Values may be sent and summed in bfloat16 or wider, within the bound.
A program may use at most 64 MiB of HBM per device.

v0:
```python
import jax
import jax.numpy as jnp
from jax import lax
from jax.sharding import PartitionSpec as P


def swapped(block, axis, distance):
    count = lax.axis_size(axis)
    route = []
    for low in range(count):
        high = low | 1 << distance
        if high != low and high < count:
            route += [(low, high), (high, low)]
    return lax.ppermute(block, axis, route)


def move_block(values, bit_number):
    return swapped(values, "dp", bit_number)


def send_back(values, bit_number):
    return swapped(values, "dp", bit_number)


def per_device(image_rows, text_rows, logit_scale, logit_bias):
    row_count = image_rows.shape[0]
    group_rows = row_count * lax.axis_size("rows")
    lower_bit = lax.axis_size("dp").bit_length() - 3
    upper_bit = lower_bit + 1
    temper = logit_scale[0]
    offset = logit_bias[0]
    gathered = lax.all_gather(text_rows, "rows", axis=0, tiled=True)
    block_one = move_block(gathered, lower_bit)
    block_two = move_block(gathered, upper_bit)
    block_three = move_block(block_one, upper_bit)
    blocks = [gathered, block_one, block_two, block_three]
    columns = lax.broadcasted_iota(jnp.int32, (row_count, group_rows), 1)
    row_place = (
        lax.broadcasted_iota(jnp.int32, (row_count, group_rows), 0)
        + lax.axis_index("rows") * row_count
    )
    diagonal = (columns == row_place).astype(jnp.float32)
    image_total = jnp.zeros((row_count, image_rows.shape[1]), jnp.float32)
    partials = []
    for round_index, current in enumerate(blocks):
        logits = (
            temper
            * lax.dot_general(
                image_rows, current, (((1,), (1,)), ((), ())), preferred_element_type=jnp.float32
            )
            + offset
        )
        weights = jax.nn.sigmoid(logits)
        if round_index == 0:
            weights = weights - diagonal
        weights = weights.astype(jnp.bfloat16)
        image_total = image_total + jnp.dot(weights, current, preferred_element_type=jnp.float32)
        product = lax.dot_general(
            weights, image_rows, (((0,), (0,)), ((), ())), preferred_element_type=jnp.float32
        )
        partials.append((temper * product).astype(jnp.bfloat16))
    grad_image = (temper * image_total).astype(jnp.bfloat16)
    back_one = send_back(partials[1], lower_bit)
    back_two = send_back(partials[2], upper_bit)
    back_three = send_back(send_back(partials[3], upper_bit), lower_bit)
    summed = partials[0].astype(jnp.float32) + back_one.astype(jnp.float32)
    summed = summed + back_two.astype(jnp.float32) + back_three.astype(jnp.float32)
    grad_text = lax.psum_scatter(
        summed.astype(jnp.bfloat16), "rows", scatter_dimension=0, tiled=True
    )
    return (grad_image, grad_text)


def solution(mesh):
    placed = (P(("dp", "rows"), None), P(("dp", "rows"), None), P(), P())
    return jax.shard_map(
        per_device,
        mesh=mesh,
        in_specs=placed,
        out_specs=(P(("dp", "rows"), None), P(("dp", "rows"), None)),
        check_vma=False,
    )
```

profile of v0, /device:TPU:1, one launch (start us, length us, event | category | flops | bytes accessed | tf_op | source)
XLA Modules:
  0.0 444.7 jit_solution(9379255188556873329)
XLA Ops:
  8.0 35.2 %all-gather.2.cloned.1.call-done = bf16[512,1152]{1,0:T(8,128)(2,1)} async-done(((bf16[128,1152]{1,0:T(8,128)(2,1)}), bf16[512,1152]{1,0:T(8,128)(2,1)}) %all-gather.2.cloned.1.call-update) | async-done | bytes 1179664 | tf_op jit(solution)/shard_map/all_gather | solution.py:32
  43.1 4.0 collective-permute-start
  47.2 51.6 %collective-permute-done = bf16[512,1152]{1,0:T(8,128)(2,1)S(1)} collective-permute-done((bf16[512,1152]{1,0:T(8,128)(2,1)}, bf16[512,1152]{1,0:T(8,128)(2,1)S(1)}, u32[]{:S(2)}, u32[]{:S(2)}) %collective-permute-start) | collective-permute-done | bytes 1179680 | tf_op jit(solution)/shard_map/ppermute | solution.py:14
  98.7 7.6 %collective-permute-start.2 = (bf16[512,1152]{1,0:T(8,128)(2,1)S(1)}, bf16[512,1152]{1,0:T(8,128)(2,1)S(1)}, u32[]{:S(2)}, u32[]{:S(2)}) collective-permute-start(bf16[512,1152]{1,0:T(8,128)(2,1)S(1)} %collective-permute-done), channel_id=1, source_target_pairs={{0,256},{256,0},{4,260},{260,4},{8,264},{264,8},{12,268},{268,12},... | collective-permute-start | bytes 3538952 | tf_op jit(solution)/shard_map/ppermute | solution.py:14
  106.3 1.9 collective-permute-start.1
  109.6 57.1 %collective-permute-done.2 = bf16[512,1152]{1,0:T(8,128)(2,1)S(1)} collective-permute-done((bf16[512,1152]{1,0:T(8,128)(2,1)S(1)}, bf16[512,1152]{1,0:T(8,128)(2,1)S(1)}, u32[]{:S(2)}, u32[]{:S(2)}) %collective-permute-start.2) | collective-permute-done | bytes 1179680 | tf_op jit(solution)/shard_map/ppermute | solution.py:14
  168.3 7.8 %collective-permute-start.5 = (bf16[512,1152]{1,0:T(8,128)(2,1)S(1)}, bf16[512,1152]{1,0:T(8,128)(2,1)}, u32[]{:S(2)}, u32[]{:S(2)}) collective-permute-start(bf16[512,1152]{1,0:T(8,128)(2,1)S(1)} %fusion.3), channel_id=1, source_target_pairs={{0,256},{256,0},{4,260},{260,4},{8,264},{264,8},{12,268},{268,12},... | collective-permute-start | bytes 3538952 | tf_op jit(solution)/shard_map/ppermute | solution.py:14
  176.1 55.5 %collective-permute-done.1 = bf16[512,1152]{1,0:T(8,128)(2,1)S(1)} collective-permute-done((bf16[512,1152]{1,0:T(8,128)(2,1)}, bf16[512,1152]{1,0:T(8,128)(2,1)S(1)}, u32[]{:S(2)}, u32[]{:S(2)}) %collective-permute-start.1) | collective-permute-done | bytes 1179680 | tf_op jit(solution)/shard_map/ppermute | solution.py:14
  232.7 1.6 fusion.2
  234.2 7.9 %collective-permute-start.4 = (bf16[512,1152]{1,0:T(8,128)(2,1)}, bf16[512,1152]{1,0:T(8,128)(2,1)S(1)}, u32[]{:S(2)}, u32[]{:S(2)}) collective-permute-start(bf16[512,1152]{1,0:T(8,128)(2,1)} %fusion.2), channel_id=1, source_target_pairs={{0,256},{256,0},{4,260},{260,4},{8,264},{264,8},{12,268},{268,12},... | collective-permute-start | bytes 3538952 | tf_op jit(solution)/shard_map/ppermute | solution.py:14
  242.7 1.6 fusion.1
  244.3 1.9 collective-permute-start.3
  246.2 38.3 %collective-permute-done.5 = bf16[512,1152]{1,0:T(8,128)(2,1)} collective-permute-done((bf16[512,1152]{1,0:T(8,128)(2,1)S(1)}, bf16[512,1152]{1,0:T(8,128)(2,1)}, u32[]{:S(2)}, u32[]{:S(2)}) %collective-permute-start.5) | collective-permute-done | bytes 1179680 | tf_op jit(solution)/shard_map/ppermute | solution.py:14
  284.5 1.9 collective-permute-start.6
  286.5 1.8 fusion.28
  288.8 20.9 %collective-permute-done.4 = bf16[512,1152]{1,0:T(8,128)(2,1)S(1)} collective-permute-done((bf16[512,1152]{1,0:T(8,128)(2,1)}, bf16[512,1152]{1,0:T(8,128)(2,1)S(1)}, u32[]{:S(2)}, u32[]{:S(2)}) %collective-permute-start.4) | collective-permute-done | bytes 1179680 | tf_op jit(solution)/shard_map/ppermute | solution.py:14
  309.7 76.0 %collective-permute-done.3 = bf16[512,1152]{1,0:T(8,128)(2,1)S(1)} collective-permute-done((bf16[512,1152]{1,0:T(8,128)(2,1)}, bf16[512,1152]{1,0:T(8,128)(2,1)S(1)}, u32[]{:S(2)}, u32[]{:S(2)}) %collective-permute-start.3) | collective-permute-done | bytes 1179680 | tf_op jit(solution)/shard_map/ppermute | solution.py:14
  385.7 25.4 %collective-permute-done.6 = bf16[512,1152]{1,0:T(8,128)(2,1)} collective-permute-done((bf16[512,1152]{1,0:T(8,128)(2,1)}, bf16[512,1152]{1,0:T(8,128)(2,1)}, u32[]{:S(2)}, u32[]{:S(2)}) %collective-permute-start.6) | collective-permute-done | bytes 1179680 | tf_op jit(solution)/shard_map/ppermute | solution.py:14
  411.1 2.8 add_convert_fusion
  414.0 1.2 copy-done.7
  415.6 0.9 copy-done.4
  418.1 0.9 copy-done.2
  419.0 1.1 fusion.6
  420.1 17.7 %reduce-scatter.2.cloned.1.call-done = bf16[128,1152]{1,0:T(8,128)(2,1)} async-done(((bf16[512,1152]{1,0:T(8,128)(2,1)}), bf16[128,1152]{1,0:T(8,128)(2,1)}) %reduce-scatter.2.cloned.1.call-update) | async-done | bytes 294928 | tf_op jit(solution)/shard_map/reduce_scatter | solution.py:68
  (26 shorter events, 6.4 us)
Async XLA Ops:
  7.2 159.6 %copy-start = (bf16[128,1152]{1,0:T(8,128)(2,1)S(1)}, bf16[128,1152]{1,0:T(8,128)(2,1)}, u32[]{:S(2)}) copy-start(bf16[128,1152]{1,0:T(8,128)(2,1)} %param.4) | copy-start | bytes 884740
  7.2 35.9 %all-gather.2.cloned.1.call-start = ((), (), s32[]{:S(2)}) async-start(), calls=%async_computation.1 | async-start | bytes 1474560 | tf_op jit(solution)/shard_map/all_gather | solution.py:32
  7.9 429.9 %reduce-scatter.2.cloned.1.call-start = ((), (), s32[]{:S(2)}) async-start(), calls=%async_computation.2 | async-start | bytes 1474560 | tf_op jit(solution)/shard_map/reduce_scatter | solution.py:68
  43.1 55.6 %collective-permute-start = (bf16[512,1152]{1,0:T(8,128)(2,1)}, bf16[512,1152]{1,0:T(8,128)(2,1)S(1)}, u32[]{:S(2)}, u32[]{:S(2)}) collective-permute-start(bf16[512,1152]{1,0:T(8,128)(2,1)} %all-gather.2.cloned.1.call-done), channel_id=1, source_target_pairs={{0,128},{128,0},{4,132},{132,4},{8,136},{136,8},{12,140},{140,12},... | collective-permute-start | bytes 3538952 | tf_op jit(solution)/shard_map/ppermute | solution.py:14
  98.7 143.4 %copy-start.3 = (bf16[512,1152]{1,0:T(8,128)(2,1)}, bf16[512,1152]{1,0:T(8,128)(2,1)S(1)}, u32[]{:S(2)}) copy-start(bf16[512,1152]{1,0:T(8,128)(2,1)S(1)} %collective-permute-done) | copy-start | bytes 3538948
  98.7 68.0 %collective-permute-start.2 = (bf16[512,1152]{1,0:T(8,128)(2,1)S(1)}, bf16[512,1152]{1,0:T(8,128)(2,1)S(1)}, u32[]{:S(2)}, u32[]{:S(2)}) collective-permute-start(bf16[512,1152]{1,0:T(8,128)(2,1)S(1)} %collective-permute-done), channel_id=1, source_target_pairs={{0,256},{256,0},{4,260},{260,4},{8,264},{264,8},{12,268},{268,12},... | collective-permute-start | bytes 3538952 | tf_op jit(solution)/shard_map/ppermute | solution.py:14
  106.3 125.3 %collective-permute-start.1 = (bf16[512,1152]{1,0:T(8,128)(2,1)}, bf16[512,1152]{1,0:T(8,128)(2,1)S(1)}, u32[]{:S(2)}, u32[]{:S(2)}) collective-permute-start(bf16[512,1152]{1,0:T(8,128)(2,1)} %all-gather.2.cloned.1.call-done), channel_id=1, source_target_pairs={{0,256},{256,0},{4,260},{260,4},{8,264},{264,8},{12,268},{268,12},... | collective-permute-start | bytes 3538952 | tf_op jit(solution)/shard_map/ppermute | solution.py:14
  166.7 1.1 copy-start.1
  168.3 116.3 %collective-permute-start.5 = (bf16[512,1152]{1,0:T(8,128)(2,1)S(1)}, bf16[512,1152]{1,0:T(8,128)(2,1)}, u32[]{:S(2)}, u32[]{:S(2)}) collective-permute-start(bf16[512,1152]{1,0:T(8,128)(2,1)S(1)} %fusion.3), channel_id=1, source_target_pairs={{0,256},{256,0},{4,260},{260,4},{8,264},{264,8},{12,268},{268,12},... | collective-permute-start | bytes 3538952 | tf_op jit(solution)/shard_map/ppermute | solution.py:14
  231.6 1.0 copy-start.5
  234.2 75.5 %collective-permute-start.4 = (bf16[512,1152]{1,0:T(8,128)(2,1)}, bf16[512,1152]{1,0:T(8,128)(2,1)S(1)}, u32[]{:S(2)}, u32[]{:S(2)}) collective-permute-start(bf16[512,1152]{1,0:T(8,128)(2,1)} %fusion.2), channel_id=1, source_target_pairs={{0,256},{256,0},{4,260},{260,4},{8,264},{264,8},{12,268},{268,12},... | collective-permute-start | bytes 3538952 | tf_op jit(solution)/shard_map/ppermute | solution.py:14
  244.3 141.4 %collective-permute-start.3 = (bf16[512,1152]{1,0:T(8,128)(2,1)}, bf16[512,1152]{1,0:T(8,128)(2,1)S(1)}, u32[]{:S(2)}, u32[]{:S(2)}) collective-permute-start(bf16[512,1152]{1,0:T(8,128)(2,1)} %fusion.1), channel_id=1, source_target_pairs={{0,128},{128,0},{4,132},{132,4},{8,136},{136,8},{12,140},{140,12},... | collective-permute-start | bytes 3538952 | tf_op jit(solution)/shard_map/ppermute | solution.py:14
  284.5 126.6 %collective-permute-start.6 = (bf16[512,1152]{1,0:T(8,128)(2,1)}, bf16[512,1152]{1,0:T(8,128)(2,1)}, u32[]{:S(2)}, u32[]{:S(2)}) collective-permute-start(bf16[512,1152]{1,0:T(8,128)(2,1)} %collective-permute-done.5), channel_id=1, source_target_pairs={{0,128},{128,0},{4,132},{132,4},{8,136},{136,8},{12,140},{140,12},... | collective-permute-start | bytes 3538952 | tf_op jit(solution)/shard_map/ppermute | solution.py:14
  413.9 1.3 copy-start.7
  415.2 1.3 copy-start.4
  416.5 1.3 copy-start.6
  417.7 1.3 copy-start.2
Sparse Core Ops, SparseCore 0:
  10.1 32.9 all-gather.1
  414.1 23.7 reduce-scatter.1
where the time goes:
time: 445 us
  waiting for transfers between devices  379 us (85%)
  starting transfers between devices  33.2 us (7%)
  between operations  15.5 us (3%)
  matrix products  9.76 us (2%)
  local copies, waits for them, and re-layouts  4.95 us (1%)
    ppermute x7, waiting for transfers between devices, swapped(): return lax.ppermute(block, axis, route)  325 us
    all_gather x1, waiting for transfers between devices, per_device(): gathered = lax.all_gather(text_rows, 'rows', axis=0, tiled=True)  35.2 us
    ppermute x7, starting transfers between devices, swapped(): return lax.ppermute(block, axis, route)  33.1 us
    reduce_scatter x1, waiting for transfers between devices, per_device(): lax.psum_scatter(summed.astype(jnp.bfloat16), 'rows', scatter_dimension=0...  17.7 us
  transfers between devices with their start and end apart: 9, of which 9 were waited for; matrix products, arithmetic and copies ran while one was open for 2% of the time, Pallas kernels for 0%

commit v1 on v0

v1 whole, which is shorter than its diff:
```python
import functools

import jax
import jax.numpy as jnp
from jax import lax
from jax.experimental import pallas as pl
from jax.experimental.pallas import tpu as pltpu
from jax.sharding import PartitionSpec as P

MESH = pl.DeviceIdType.MESH
CHUNKS = 4
F32 = jnp.float32
BF16 = jnp.bfloat16

I_CORE, I_Y, I_FWD, T_Z, T_Y, T_FWD = range(6)


def sigmoid(x):
    return 1.0 / (1.0 + jnp.exp(-x))


def kernel(
    quarter, rows, scale_ref, bias_ref, image_ref, text_ref, grad_image_ref, grad_text_ref,
    images, texts, weights, image_acc, text_acc, out_bf, staged, landed,
    send_sem, recv_sem, back_send, back_recv, local_sem, out_sem,
):
    dp, row = lax.axis_index("dp"), lax.axis_index("rows")
    low = quarter - 2 * quarter * ((dp // quarter) % 2)
    high = 2 * quarter - 4 * quarter * ((dp // (2 * quarter)) % 2)
    to_y2 = {"dp": dp + low, "rows": row}
    to_y6 = {"dp": dp + low + high, "rows": row}
    to_core = {"dp": dp, "rows": row + 1 - 2 * (row % 2)}
    to_z = {"dp": dp, "rows": row + 2 - 4 * (row // 2)}
    partner = {I_CORE: to_core, I_Y: to_y2, I_FWD: to_core, T_Z: to_z, T_Y: to_y6, T_FWD: to_z}
    part = rows // CHUNKS

    load_i = pltpu.make_async_copy(image_ref, images.at[pl.ds(0, rows)], local_sem.at[0])
    load_t = pltpu.make_async_copy(text_ref, texts.at[pl.ds(0, rows)], local_sem.at[1])
    load_i.start()
    load_t.start()
    barrier = pltpu.get_barrier_semaphore()
    for other in (to_y2, to_y6, to_core, to_z):
        pl.semaphore_signal(barrier, inc=1, device_id=other, device_id_type=MESH)
    pl.semaphore_wait(barrier, 4)
    load_i.wait()
    load_t.wait()

    def gather(stream, k):
        held = images if stream < T_Z else texts
        source = {I_CORE: 0, I_Y: 0, I_FWD: 2, T_Z: 0, T_Y: 0, T_FWD: 2}[stream]
        target = {I_CORE: 1, I_Y: 2, I_FWD: 3, T_Z: 1, T_Y: 2, T_FWD: 3}[stream]
        return pltpu.make_async_remote_copy(
            src_ref=held.at[pl.ds(source * rows + k * part, part)],
            dst_ref=held.at[pl.ds(target * rows + k * part, part)],
            send_sem=send_sem.at[stream, k],
            recv_sem=recv_sem.at[stream, k],
            device_id=partner[stream],
            device_id_type=MESH,
        )

    def back(stream, k):
        return pltpu.make_async_remote_copy(
            src_ref=staged.at[stream, pl.ds(k * part, part)],
            dst_ref=landed.at[stream, pl.ds(k * part, part)],
            send_sem=back_send.at[stream, k],
            recv_sem=back_recv.at[stream, k],
            device_id=partner[stream],
            device_id_type=MESH,
        )

    scale = scale_ref[0]
    bias = bias_ref[0]

    def fill_weights(i0, i1, t0, t1):
        block = lax.dot_general(
            images[pl.ds(i0 * rows, (i1 - i0) * rows)],
            texts[pl.ds(t0 * rows, (t1 - t0) * rows)],
            (((1,), (1,)), ((), ())),
            preferred_element_type=F32,
        )
        block = sigmoid(scale * block + bias)
        if i0 == 0 and t0 == 0:
            r = lax.broadcasted_iota(jnp.int32, block.shape, 0)
            c = lax.broadcasted_iota(jnp.int32, block.shape, 1)
            block = block - jnp.where((r == c) & (r < rows), 1.0, 0.0)
        weights[pl.ds(i0 * rows, (i1 - i0) * rows), pl.ds(t0 * rows, (t1 - t0) * rows)] = block.astype(BF16)

    def image_grad(i):
        return scale * jnp.dot(weights[pl.ds(i * rows, rows), :], texts[...], preferred_element_type=F32)

    def text_grad(t):
        return scale * lax.dot_general(
            weights[:, pl.ds(t * rows, rows)], images[...], (((0,), (0,)), ((), ())), preferred_element_type=F32
        )

    for k in range(CHUNKS):
        gather(I_Y, k).start()
        gather(T_Y, k).start()
        gather(T_Z, k).start()
        gather(I_CORE, k).start()
    for k in range(CHUNKS):
        gather(I_Y, k).wait_recv()
        gather(I_FWD, k).start()
        gather(T_Y, k).wait_recv()
        gather(T_FWD, k).start()
        if k == CHUNKS - 2:
            for j in range(CHUNKS):
                gather(I_CORE, j).wait_recv()
                gather(T_Z, j).wait_recv()
            fill_weights(0, 2, 0, 2)
    for k in range(CHUNKS):
        gather(I_FWD, k).wait_recv()
    fill_weights(2, 4, 0, 2)
    for k in range(CHUNKS):
        gather(T_FWD, k).wait_recv()
    fill_weights(0, 4, 2, 4)

    staged[T_FWD] = text_grad(3).astype(BF16)
    for k in range(CHUNKS):
        back(T_FWD, k).start()
    staged[I_FWD] = image_grad(3).astype(BF16)
    for k in range(CHUNKS):
        back(I_FWD, k).start()
    image_acc[...] = image_grad(2)
    for k in range(CHUNKS):
        back(I_FWD, k).wait_recv()
        at = pl.ds(k * part, part)
        staged[I_Y, at] = (image_acc[at] + landed[I_FWD, at].astype(F32)).astype(BF16)
        back(I_Y, k).start()
    text_acc[...] = text_grad(2)
    staged[T_Z] = text_grad(1).astype(BF16)
    for k in range(CHUNKS):
        back(T_FWD, k).wait_recv()
        at = pl.ds(k * part, part)
        staged[T_Y, at] = (text_acc[at] + landed[T_FWD, at].astype(F32)).astype(BF16)
        back(T_Y, k).start()
        back(T_Z, k).start()
    staged[I_CORE] = image_grad(1).astype(BF16)
    for k in range(CHUNKS):
        back(I_CORE, k).start()
    image_acc[...] = image_grad(0)
    text_acc[...] = text_grad(0)
    for k in range(CHUNKS):
        at = pl.ds(k * part, part)
        back(I_CORE, k).wait_recv()
        back(T_Z, k).wait_recv()
        image_acc[at] = image_acc[at] + landed[I_CORE, at].astype(F32)
        text_acc[at] = text_acc[at] + landed[T_Z, at].astype(F32)
    for k in range(CHUNKS):
        at = pl.ds(k * part, part)
        back(I_Y, k).wait_recv()
        out_bf[0, at] = (image_acc[at] + landed[I_Y, at].astype(F32)).astype(BF16)
        pltpu.make_async_copy(out_bf.at[0, at], grad_image_ref.at[at], out_sem.at[0, k]).start()
        back(T_Y, k).wait_recv()
        out_bf[1, at] = (text_acc[at] + landed[T_Y, at].astype(F32)).astype(BF16)
        pltpu.make_async_copy(out_bf.at[1, at], grad_text_ref.at[at], out_sem.at[1, k]).start()
    for stream in range(6):
        for k in range(CHUNKS):
            gather(stream, k).wait_send()
            back(stream, k).wait_send()
    for k in range(CHUNKS):
        at = pl.ds(k * part, part)
        pltpu.make_async_copy(out_bf.at[0, at], grad_image_ref.at[at], out_sem.at[0, k]).wait()
        pltpu.make_async_copy(out_bf.at[1, at], grad_text_ref.at[at], out_sem.at[1, k]).wait()


def per_device(image_rows, text_rows, logit_scale, logit_bias):
    rows, width = image_rows.shape
    quarter = lax.axis_size("dp") // 4
    shape = jax.ShapeDtypeStruct((rows, width), BF16)
    smem = pl.BlockSpec(memory_space=pltpu.SMEM)
    hbm = pl.BlockSpec(memory_space=pl.ANY)
    dma = pltpu.SemaphoreType.DMA
    return pl.pallas_call(
        functools.partial(kernel, quarter, rows),
        out_shape=(shape, shape),
        in_specs=[smem, smem, hbm, hbm],
        out_specs=(hbm, hbm),
        scratch_shapes=[
            pltpu.VMEM((4 * rows, width), BF16),
            pltpu.VMEM((4 * rows, width), BF16),
            pltpu.VMEM((4 * rows, 4 * rows), BF16),
            pltpu.VMEM((rows, width), F32),
            pltpu.VMEM((rows, width), F32),
            pltpu.VMEM((2, rows, width), BF16),
            pltpu.VMEM((6, rows, width), BF16),
            pltpu.VMEM((6, rows, width), BF16),
            dma((6, CHUNKS)),
            dma((6, CHUNKS)),
            dma((6, CHUNKS)),
            dma((6, CHUNKS)),
            dma((2,)),
            dma((2, CHUNKS)),
        ],
        compiler_params=pltpu.CompilerParams(
            collective_id=0, has_side_effects=True, vmem_limit_bytes=48 * 1024 * 1024
        ),
        cost_estimate=pl.CostEstimate(
            flops=6 * rows * rows * 16 * width, bytes_accessed=8 * rows * width, transcendentals=16 * rows * rows
        ),
        name="contrastive",
    )(logit_scale, logit_bias, image_rows, text_rows)


def solution(mesh):
    split = P(("dp", "rows"), None)
    return jax.shard_map(
        per_device,
        mesh=mesh,
        in_specs=(split, split, P(), P()),
        out_specs=(split, split),
        check_vma=False,
    )
```

time: 445 us -> 51.3 us (0.12)
  waiting for transfers between devices: 379 us -> 0 us
  Pallas kernels: 0 us -> 45.8 us
  starting transfers between devices: 33.2 us -> 0 us
  between operations: 15.5 us -> 1.94 us
  matrix products: 9.76 us -> 0 us
    ppermute x7 -> x0, waiting for transfers between devices: 325 us -> none  [swapped(): return lax.ppermute(block, axis, route)]
    pallas_call x0 -> x1, Pallas kernels: none -> 45.8 us  [per_device(): pl.pallas_call(functools.partial(kernel, quarter, rows), out_shape=(shape...]
    all_gather x1 -> x0, waiting for transfers between devices: 35.2 us -> none  [per_device(): gathered = lax.all_gather(text_rows, 'rows', axis=0, tiled=True)]
    ppermute x7 -> x0, starting transfers between devices: 33.1 us -> none  [swapped(): return lax.ppermute(block, axis, route)]
    reduce_scatter x1 -> x0, waiting for transfers between devices: 17.7 us -> none  [per_device(): lax.psum_scatter(summed.astype(jnp.bfloat16), 'rows', scatter_dimension=0...]
    dot_general x12 -> x0, matrix products: 9.76 us -> none  [the longest x4 4.11 us: per_device(): lax.dot_general(weights, image_rows, (((0,), (0,)), ((), ())), preferred_...]
  transfers between devices with their start and end apart: 9 -> 0, of which waited for: 9 -> 0; matrix products, arithmetic and copies ran while one was open for 2% -> 0% of each run, Pallas kernels for 0% -> 0%
where the time goes in v1:
time: 51.3 us; the launch traced here: 51.1 us
  Pallas kernels  45.8 us (89%)
  local copies, waits for them, and re-layouts  3.35 us (7%)
  between operations  1.94 us (4%)
    pallas_call x1, Pallas kernels, per_device(): pl.pallas_call(functools.partial(kernel, quarter, rows), out_shape=(shape...  45.8 us
    unnamed x6, local copies, waits for them, and re-layouts  3.35 us

profile of v1, /device:TPU:1, one launch (start us, length us, event | category | flops | bytes accessed | tf_op | source)
XLA Modules:
  0.0 51.1 jit_solution(2909241142673915933)
XLA Ops:
  1.9 0.0 copy-start
  1.9 1.0 %copy-done = bf16[128,1152]{1,0:T(8,128)(2,1)S(1)} copy-done((bf16[128,1152]{1,0:T(8,128)(2,1)S(1)}, bf16[128,1152]{1,0:T(8,128)(2,1)}, u32[]{:S(2)}) %copy-start) | copy-done | bytes 294936
  2.9 0.0 copy-start.1
  2.9 1.0 %copy-done.1 = bf16[128,1152]{1,0:T(8,128)(2,1)S(1)} copy-done((bf16[128,1152]{1,0:T(8,128)(2,1)S(1)}, bf16[128,1152]{1,0:T(8,128)(2,1)}, u32[]{:S(2)}) %copy-start.1) | copy-done | bytes 294936
  3.8 45.8 %contrastive.1 = (bf16[128,1152]{1,0:T(8,128)(2,1)S(1)}, bf16[128,1152]{1,0:T(8,128)(2,1)S(1)}) custom-call(f32[1]{0:T(128)S(6)} %copy.8.scale_ref, f32[1]{0:T(128)S(6)} %copy.9.bias_ref, bf16[128,1152]{1,0:T(8,128)(2,1)S(1)} %copy-done, bf16[128,1152]{1,0:T(8,128)(2,1)S(1)} %copy-done.1), custom_call_target="tpu_custom_call" | custom-call | flops 1811939328 | bytes 1179648 | tf_op jit(solution)/shard_map/contrastive/pallas_call | solution.py:174
  49.7 0.7 %copy.10 = bf16[128,1152]{1,0:T(8,128)(2,1)} copy(bf16[128,1152]{1,0:T(8,128)(2,1)S(1)} %get-tuple-element.4) | data formatting | bytes 589824
  50.4 0.7 %copy.11 = bf16[128,1152]{1,0:T(8,128)(2,1)} copy(bf16[128,1152]{1,0:T(8,128)(2,1)S(1)} %get-tuple-element.5) | data formatting | bytes 589824
Async XLA Ops:
  1.9 1.0 %copy-start = (bf16[128,1152]{1,0:T(8,128)(2,1)S(1)}, bf16[128,1152]{1,0:T(8,128)(2,1)}, u32[]{:S(2)}) copy-start(bf16[128,1152]{1,0:T(8,128)(2,1)} %image_ref.1) | copy-start | bytes 884740
  2.9 1.0 %copy-start.1 = (bf16[128,1152]{1,0:T(8,128)(2,1)S(1)}, bf16[128,1152]{1,0:T(8,128)(2,1)}, u32[]{:S(2)}) copy-start(bf16[128,1152]{1,0:T(8,128)(2,1)} %text_ref.1) | copy-start | bytes 884740

commit v2 on v1

--- a/solution.py
+++ b/solution.py
@@ -21,8 +21,8 @@
 
 def kernel(
     quarter, rows, scale_ref, bias_ref, image_ref, text_ref, grad_image_ref, grad_text_ref,
-    images, texts, weights, image_acc, text_acc, out_bf, staged, landed,
-    send_sem, recv_sem, back_send, back_recv, local_sem, out_sem,
+    images, texts, weights, image_acc, text_acc, staged, landed,
+    send_sem, recv_sem, back_send, back_recv, local_sem,
 ):
     dp, row = lax.axis_index("dp"), lax.axis_index("rows")
     low = quarter - 2 * quarter * ((dp // quarter) % 2)
@@ -149,40 +149,44 @@
     for k in range(CHUNKS):
         at = pl.ds(k * part, part)
         back(I_Y, k).wait_recv()
-        out_bf[0, at] = (image_acc[at] + landed[I_Y, at].astype(F32)).astype(BF16)
-        pltpu.make_async_copy(out_bf.at[0, at], grad_image_ref.at[at], out_sem.at[0, k]).start()
+        grad_image_ref[at] = (image_acc[at] + landed[I_Y, at].astype(F32)).astype(BF16)
         back(T_Y, k).wait_recv()
-        out_bf[1, at] = (text_acc[at] + landed[T_Y, at].astype(F32)).astype(BF16)
-        pltpu.make_async_copy(out_bf.at[1, at], grad_text_ref.at[at], out_sem.at[1, k]).start()
+        grad_text_ref[at] = (text_acc[at] + landed[T_Y, at].astype(F32)).astype(BF16)
     for stream in range(6):
         for k in range(CHUNKS):
             gather(stream, k).wait_send()
             back(stream, k).wait_send()
-    for k in range(CHUNKS):
-        at = pl.ds(k * part, part)
-        pltpu.make_async_copy(out_bf.at[0, at], grad_image_ref.at[at], out_sem.at[0, k]).wait()
-        pltpu.make_async_copy(out_bf.at[1, at], grad_text_ref.at[at], out_sem.at[1, k]).wait()
+
+def write_out(image_ref, text_ref, grad_image_ref, grad_text_ref, sem):
+    copies = [
+        pltpu.make_async_copy(image_ref, grad_image_ref, sem.at[0]),
+        pltpu.make_async_copy(text_ref, grad_text_ref, sem.at[1]),
+    ]
+    for copy in copies:
+        copy.start()
+    for copy in copies:
+        copy.wait()
 
 
 def per_device(image_rows, text_rows, logit_scale, logit_bias):
     rows, width = image_rows.shape
     quarter = lax.axis_size("dp") // 4
     shape = jax.ShapeDtypeStruct((rows, width), BF16)
+    vmem = pl.BlockSpec(memory_space=pltpu.VMEM)
+    hbm = pl.BlockSpec(memory_space=pltpu.HBM)
     smem = pl.BlockSpec(memory_space=pltpu.SMEM)
-    hbm = pl.BlockSpec(memory_space=pl.ANY)
     dma = pltpu.SemaphoreType.DMA
-    return pl.pallas_call(
+    sums = pl.pallas_call(
         functools.partial(kernel, quarter, rows),
-        out_shape=(shape, shape),
+        out_shape=(pltpu.VMEM((rows, width), BF16), pltpu.VMEM((rows, width), BF16)),
         in_specs=[smem, smem, hbm, hbm],
-        out_specs=(hbm, hbm),
+        out_specs=(vmem, vmem),
         scratch_shapes=[
             pltpu.VMEM((4 * rows, width), BF16),
             pltpu.VMEM((4 * rows, width), BF16),
             pltpu.VMEM((4 * rows, 4 * rows), BF16),
             pltpu.VMEM((rows, width), F32),
             pltpu.VMEM((rows, width), F32),
-            pltpu.VMEM((2, rows, width), BF16),
             pltpu.VMEM((6, rows, width), BF16),
             pltpu.VMEM((6, rows, width), BF16),
             dma((6, CHUNKS)),
@@ -190,7 +194,6 @@
             dma((6, CHUNKS)),
             dma((6, CHUNKS)),
             dma((2,)),
-            dma((2, CHUNKS)),
         ],
         compiler_params=pltpu.CompilerParams(
             collective_id=0, has_side_effects=True, vmem_limit_bytes=48 * 1024 * 1024
@@ -199,7 +202,16 @@
             flops=6 * rows * rows * 16 * width, bytes_accessed=8 * rows * width, transcendentals=16 * rows * rows
         ),
         name="contrastive",
-    )(logit_scale, logit_bias, image_rows, text_rows)
+    )(logit_scale, logit_bias, *(pltpu.with_memory_space_constraint(a, pltpu.HBM) for a in (image_rows, text_rows)))
+    return pl.pallas_call(
+        write_out,
+        out_shape=(shape, shape),
+        in_specs=[vmem, vmem],
+        out_specs=(hbm, hbm),
+        scratch_shapes=[dma((2,))],
+        compiler_params=pltpu.CompilerParams(vmem_limit_bytes=4 * 1024 * 1024),
+        name="write_out",
+    )(*sums)
 
 
 def solution(mesh):

time: 51.3 us -> 47.8 us (0.932)
  local copies, waits for them, and re-layouts: 3.35 us -> 0 us
    unnamed x6 -> x0, local copies, waits for them, and re-layouts: 3.35 us -> none
    pallas_call x1 -> x2, Pallas kernels: 45.8 us -> 45.7 us  [the longest x1 44.8 us: per_device(): pl.pallas_call(functools.partial(kernel, quarter, rows), out_shape=(pltpu...]
where the time goes in v2:
time: 47.8 us; the launch traced here: 47.6 us
  Pallas kernels  45.7 us (96%)
  between operations  1.93 us (4%)
    pallas_call x1, Pallas kernels, per_device(): pl.pallas_call(functools.partial(kernel, quarter, rows), out_shape=(pltpu...  44.8 us

profile of v2, /device:TPU:1, one launch (start us, length us, event | category | flops | bytes accessed | tf_op | source)
XLA Modules:
  0.0 47.6 jit_solution(10634566957729950571)
XLA Ops:
  1.9 44.8 %contrastive.1 = (bf16[128,1152]{1,0:T(8,128)(2,1)S(1)}, bf16[128,1152]{1,0:T(8,128)(2,1)S(1)}) custom-call(f32[1]{0:T(128)S(6)} %copy.6.scale_ref, f32[1]{0:T(128)S(6)} %copy.7.bias_ref, bf16[128,1152]{1,0:T(8,128)(2,1)} %image_ref.1, bf16[128,1152]{1,0:T(8,128)(2,1)} %text_ref.1), custom_call_target="tpu_custom_call" | custom-call | flops 1811939328 | bytes 1179648 | tf_op jit(solution)/shard_map/contrastive/pallas_call | solution.py:179
  46.8 0.8 %write_out.1 = (bf16[128,1152]{1,0:T(8,128)(2,1)}, bf16[128,1152]{1,0:T(8,128)(2,1)}) custom-call(bf16[128,1152]{1,0:T(8,128)(2,1)S(1)} %get-tuple-element.4.image_ref, bf16[128,1152]{1,0:T(8,128)(2,1)S(1)} %get-tuple-element.5.text_ref), custom_call_target="tpu_custom_call" | custom-call | tf_op jit(solution)/shard_map/write_out/pallas_call | solution.py:206

commit v3 on v2

--- a/solution.py
+++ b/solution.py
@@ -9,6 +9,7 @@
 
 MESH = pl.DeviceIdType.MESH
 CHUNKS = 4
+LEAD = 4
 F32 = jnp.float32
 BF16 = jnp.bfloat16
 
@@ -93,11 +94,25 @@
             weights[:, pl.ds(t * rows, rows)], images[...], (((0,), (0,)), ((), ())), preferred_element_type=F32
         )
 
-    for k in range(CHUNKS):
-        gather(I_Y, k).start()
-        gather(T_Y, k).start()
+    odd = (dp // (quarter // 2)) % 2
+
+    @pl.when(odd == 0)
+    def _():
+        for k in range(CHUNKS):
+            gather(I_Y, k).start()
+            gather(T_Y, k).start()
+
+    for k in range(CHUNKS):
         gather(T_Z, k).start()
         gather(I_CORE, k).start()
+
+    @pl.when(odd == 1)
+    def _():
+        for k in range(LEAD):
+            gather(T_Z, k).wait_recv()
+        for k in range(CHUNKS):
+            gather(I_Y, k).start()
+            gather(T_Y, k).start()
     for k in range(CHUNKS):
         gather(I_Y, k).wait_recv()
         gather(I_FWD, k).start()
@@ -106,7 +121,14 @@
         if k == CHUNKS - 2:
             for j in range(CHUNKS):
                 gather(I_CORE, j).wait_recv()
-                gather(T_Z, j).wait_recv()
+                if j >= LEAD:
+                    gather(T_Z, j).wait_recv()
+
+            @pl.when(odd == 0)
+            def _():
+                for j in range(LEAD):
+                    gather(T_Z, j).wait_recv()
+
             fill_weights(0, 2, 0, 2)
     for k in range(CHUNKS):
         gather(I_FWD, k).wait_recv()

time: 47.8 us -> 44.3 us (0.927)
  the two profiles are of different devices: /device:TPU:1 before, /device:TPU:132 now
where the time goes in v3:
time: 44.3 us; the launch traced here: 44.1 us
  Pallas kernels  42.2 us (95%)
  between operations  1.93 us (4%)
    pallas_call x1, Pallas kernels, per_device(): pl.pallas_call(functools.partial(kernel, quarter, rows), out_shape=(pltpu...  41.3 us

profile of v3, /device:TPU:132, one launch (start us, length us, event | category | flops | bytes accessed | tf_op | source)
XLA Modules:
  0.0 44.1 jit_solution(2665655526210325723)
XLA Ops:
  1.9 41.3 %contrastive.1 = (bf16[128,1152]{1,0:T(8,128)(2,1)S(1)}, bf16[128,1152]{1,0:T(8,128)(2,1)S(1)}) custom-call(f32[1]{0:T(128)S(6)} %copy.6.scale_ref, f32[1]{0:T(128)S(6)} %copy.7.bias_ref, bf16[128,1152]{1,0:T(8,128)(2,1)} %image_ref.1, bf16[128,1152]{1,0:T(8,128)(2,1)} %text_ref.1), custom_call_target="tpu_custom_call" | custom-call | flops 1811939328 | bytes 1179648 | tf_op jit(solution)/shard_map/contrastive/pallas_call | solution.py:201
  43.3 0.8 %write_out.1 = (bf16[128,1152]{1,0:T(8,128)(2,1)}, bf16[128,1152]{1,0:T(8,128)(2,1)}) custom-call(bf16[128,1152]{1,0:T(8,128)(2,1)S(1)} %get-tuple-element.4.image_ref, bf16[128,1152]{1,0:T(8,128)(2,1)S(1)} %get-tuple-element.5.text_ref), custom_call_target="tpu_custom_call" | custom-call | tf_op jit(solution)/shard_map/write_out/pallas_call | solution.py:228

commit v4 on v3

--- a/solution.py
+++ b/solution.py
@@ -10,6 +10,8 @@
 MESH = pl.DeviceIdType.MESH
 CHUNKS = 4
 LEAD = 4
+EARLY = 2
+AHEAD = 2
 F32 = jnp.float32
 BF16 = jnp.bfloat16
 
@@ -22,7 +24,7 @@
 
 def kernel(
     quarter, rows, scale_ref, bias_ref, image_ref, text_ref, grad_image_ref, grad_text_ref,
-    images, texts, weights, image_acc, text_acc, staged, landed,
+    images, texts, near, far, image_acc, text_acc, staged, landed,
     send_sem, recv_sem, back_send, back_recv, local_sem,
 ):
     dp, row = lax.axis_index("dp"), lax.axis_index("rows")
@@ -72,27 +74,41 @@
     scale = scale_ref[0]
     bias = bias_ref[0]
 
-    def fill_weights(i0, i1, t0, t1):
+    def fill_near(i0, i1):
         block = lax.dot_general(
-            images[pl.ds(i0 * rows, (i1 - i0) * rows)],
-            texts[pl.ds(t0 * rows, (t1 - t0) * rows)],
-            (((1,), (1,)), ((), ())),
-            preferred_element_type=F32,
+            images[pl.ds(i0 * rows, (i1 - i0) * rows)], texts[pl.ds(0, 2 * rows)], (((1,), (1,)), ((), ())), preferred_element_type=F32
         )
         block = sigmoid(scale * block + bias)
-        if i0 == 0 and t0 == 0:
+        if i0 == 0:
             r = lax.broadcasted_iota(jnp.int32, block.shape, 0)
             c = lax.broadcasted_iota(jnp.int32, block.shape, 1)
             block = block - jnp.where((r == c) & (r < rows), 1.0, 0.0)
-        weights[pl.ds(i0 * rows, (i1 - i0) * rows), pl.ds(t0 * rows, (t1 - t0) * rows)] = block.astype(BF16)
-
-    def image_grad(i):
-        return scale * jnp.dot(weights[pl.ds(i * rows, rows), :], texts[...], preferred_element_type=F32)
-
-    def text_grad(t):
+        near[pl.ds(i0 * rows, (i1 - i0) * rows)] = block.astype(BF16)
+
+    def fill_far(start, size):
+        block = lax.dot_general(
+            texts[pl.ds(2 * rows + start, size)], images[...], (((1,), (1,)), ((), ())), preferred_element_type=F32
+        )
+        far[pl.ds(start, size)] = sigmoid(scale * block + bias).astype(BF16)
+
+    def near_images(i, n):
+        return jnp.dot(near[pl.ds(i * rows, n * rows)], texts[pl.ds(0, 2 * rows)], preferred_element_type=F32)
+
+    def far_images(i, n, start, size):
+        return lax.dot_general(
+            far[pl.ds(start, size), pl.ds(i * rows, n * rows)],
+            texts[pl.ds(2 * rows + start, size)],
+            (((0,), (0,)), ((), ())),
+            preferred_element_type=F32,
+        )
+
+    def near_texts(t):
         return scale * lax.dot_general(
-            weights[:, pl.ds(t * rows, rows)], images[...], (((0,), (0,)), ((), ())), preferred_element_type=F32
-        )
+            near[:, pl.ds(t * rows, rows)], images[...], (((0,), (0,)), ((), ())), preferred_element_type=F32
+        )
+
+    def far_texts(start, size):
+        return scale * jnp.dot(far[pl.ds(start, size)], images[...], preferred_element_type=F32)
 
     odd = (dp // (quarter // 2)) % 2
 
@@ -129,55 +145,85 @@
                 for j in range(LEAD):
                     gather(T_Z, j).wait_recv()
 
-            fill_weights(0, 2, 0, 2)
+            fill_near(0, 2)
     for k in range(CHUNKS):
         gather(I_FWD, k).wait_recv()
-    fill_weights(2, 4, 0, 2)
-    for k in range(CHUNKS):
+    fill_near(2, 4)
+    staged[T_Z] = near_texts(1).astype(BF16)
+
+    @pl.when(odd == 1)
+    def _():
+        for k in range(EARLY):
+            back(T_Z, k).start()
+
+    head = rows - part
+    for k in range(CHUNKS - 1):
         gather(T_FWD, k).wait_recv()
-    fill_weights(0, 4, 2, 4)
-
-    staged[T_FWD] = text_grad(3).astype(BF16)
-    for k in range(CHUNKS):
+    fill_far(rows, head)
+    staged[T_FWD, pl.ds(0, head)] = far_texts(rows, head).astype(BF16)
+
+    for k in range(CHUNKS - 1):
         back(T_FWD, k).start()
-    staged[I_FWD] = image_grad(3).astype(BF16)
+
+    fill_far(0, rows)
+    image_acc[...] = near_images(2, 2) + far_images(2, 2, 0, rows + head)
+    text_acc[...] = far_texts(0, rows)
+    gather(T_FWD, CHUNKS - 1).wait_recv()
+
+    fill_far(rows + head, part)
+    staged[T_FWD, pl.ds(head, part)] = far_texts(rows + head, part).astype(BF16)
+    back(T_FWD, CHUNKS - 1).start()
+    image_acc[...] = scale * (image_acc[...] + far_images(2, 2, rows + head, part))
+    staged[I_FWD] = image_acc[pl.ds(rows, rows)].astype(BF16)
     for k in range(CHUNKS):
         back(I_FWD, k).start()
-    image_acc[...] = image_grad(2)
     for k in range(CHUNKS):
         back(I_FWD, k).wait_recv()
         at = pl.ds(k * part, part)
         staged[I_Y, at] = (image_acc[at] + landed[I_FWD, at].astype(F32)).astype(BF16)
         back(I_Y, k).start()
-    text_acc[...] = text_grad(2)
-    staged[T_Z] = text_grad(1).astype(BF16)
     for k in range(CHUNKS):
         back(T_FWD, k).wait_recv()
         at = pl.ds(k * part, part)
         staged[T_Y, at] = (text_acc[at] + landed[T_FWD, at].astype(F32)).astype(BF16)
         back(T_Y, k).start()
-        back(T_Z, k).start()
-    staged[I_CORE] = image_grad(1).astype(BF16)
+        if k == CHUNKS - 1 - AHEAD:
+
+            @pl.when(odd == 0)
+            def _():
+                for j in range(CHUNKS):
+                    back(T_Z, j).start()
+
+            @pl.when(odd == 1)
+            def _():
+                for j in range(EARLY, CHUNKS):
+                    back(T_Z, j).start()
+
+    staged[I_CORE] = (scale * (near_images(1, 1) + far_images(1, 1, 0, 2 * rows))).astype(BF16)
     for k in range(CHUNKS):
         back(I_CORE, k).start()
-    image_acc[...] = image_grad(0)
-    text_acc[...] = text_grad(0)
+    image_acc[pl.ds(0, rows)] = scale * (near_images(0, 1) + far_images(0, 1, 0, 2 * rows))
+    text_acc[...] = near_texts(0)
     for k in range(CHUNKS):
         at = pl.ds(k * part, part)
         back(I_CORE, k).wait_recv()
-        back(T_Z, k).wait_recv()
         image_acc[at] = image_acc[at] + landed[I_CORE, at].astype(F32)
-        text_acc[at] = text_acc[at] + landed[T_Z, at].astype(F32)
-    for k in range(CHUNKS):
-        at = pl.ds(k * part, part)
+    for k in range(CHUNKS):
+        for stream in range(6):
+            gather(stream, k).wait_send()
+        for stream in (I_CORE, I_FWD, T_FWD):
+            back(stream, k).wait_send()
+    for k in range(CHUNKS):
+        at = pl.ds(k * part, part)
+        if k == CHUNKS - 1:
+            for j in range(CHUNKS):
+                for stream in (I_Y, T_Z, T_Y):
+                    back(stream, j).wait_send()
         back(I_Y, k).wait_recv()
         grad_image_ref[at] = (image_acc[at] + landed[I_Y, at].astype(F32)).astype(BF16)
+        back(T_Z, k).wait_recv()
         back(T_Y, k).wait_recv()
-        grad_text_ref[at] = (text_acc[at] + landed[T_Y, at].astype(F32)).astype(BF16)
-    for stream in range(6):
-        for k in range(CHUNKS):
-            gather(stream, k).wait_send()
-            back(stream, k).wait_send()
+        grad_text_ref[at] = (text_acc[at] + landed[T_Z, at].astype(F32) + landed[T_Y, at].astype(F32)).astype(BF16)
 
 def write_out(image_ref, text_ref, grad_image_ref, grad_text_ref, sem):
     copies = [
@@ -206,8 +252,9 @@
         scratch_shapes=[
             pltpu.VMEM((4 * rows, width), BF16),
             pltpu.VMEM((4 * rows, width), BF16),
-            pltpu.VMEM((4 * rows, 4 * rows), BF16),
-            pltpu.VMEM((rows, width), F32),
+            pltpu.VMEM((4 * rows, 2 * rows), BF16),
+            pltpu.VMEM((2 * rows, 4 * rows), BF16),
+            pltpu.VMEM((2 * rows, width), F32),
             pltpu.VMEM((rows, width), F32),
             pltpu.VMEM((6, rows, width), BF16),
             pltpu.VMEM((6, rows, width), BF16),

time: 44.3 us -> 43.9 us (level)
  the two profiles are of different devices: /device:TPU:132 before, /device:TPU:141 now
where the time goes in v4:
time: 43.9 us; the launch traced here: 43.7 us
  Pallas kernels  41.8 us (95%)
  between operations  1.93 us (4%)
    pallas_call x1, Pallas kernels, per_device(): pl.pallas_call(functools.partial(kernel, quarter, rows), out_shape=(pltpu...  41 us

profile of v4, /device:TPU:141, one launch (start us, length us, event | category | flops | bytes accessed | tf_op | source)
XLA Modules:
  0.0 43.7 jit_solution(14286670796914274428)
XLA Ops:
  1.9 41.0 %contrastive.1 = (bf16[128,1152]{1,0:T(8,128)(2,1)S(1)}, bf16[128,1152]{1,0:T(8,128)(2,1)S(1)}) custom-call(f32[1]{0:T(128)S(6)} %copy.6.scale_ref, f32[1]{0:T(128)S(6)} %copy.7.bias_ref, bf16[128,1152]{1,0:T(8,128)(2,1)} %image_ref.1, bf16[128,1152]{1,0:T(8,128)(2,1)} %text_ref.1), custom_call_target="tpu_custom_call" | custom-call | flops 1811939328 | bytes 1179648 | tf_op jit(solution)/shard_map/contrastive/pallas_call | solution.py:247
  42.9 0.8 %write_out.1 = (bf16[128,1152]{1,0:T(8,128)(2,1)}, bf16[128,1152]{1,0:T(8,128)(2,1)}) custom-call(bf16[128,1152]{1,0:T(8,128)(2,1)S(1)} %get-tuple-element.4.image_ref, bf16[128,1152]{1,0:T(8,128)(2,1)S(1)} %get-tuple-element.5.text_ref), custom_call_target="tpu_custom_call" | custom-call | tf_op jit(solution)/shard_map/write_out/pallas_call | solution.py:275

commit v5 on v4

--- a/solution.py
+++ b/solution.py
@@ -10,7 +10,8 @@
 MESH = pl.DeviceIdType.MESH
 CHUNKS = 4
 LEAD = 4
-EARLY = 2
+EARLY = 1
+ACROSS = 1
 AHEAD = 2
 F32 = jnp.float32
 BF16 = jnp.bfloat16
@@ -71,6 +72,16 @@
             device_id_type=MESH,
         )
 
+    def across(k):
+        return pltpu.make_async_remote_copy(
+            src_ref=texts.at[pl.ds(rows + k * part, part)],
+            dst_ref=texts.at[pl.ds(3 * rows + k * part, part)],
+            send_sem=send_sem.at[T_FWD, k],
+            recv_sem=recv_sem.at[T_FWD, k],
+            device_id=to_y6,
+            device_id_type=MESH,
+        )
+
     scale = scale_ref[0]
     bias = bias_ref[0]
 
@@ -129,11 +140,20 @@
         for k in range(CHUNKS):
             gather(I_Y, k).start()
             gather(T_Y, k).start()
+        for k in range(CHUNKS - ACROSS, CHUNKS):
+            across(k).start()
     for k in range(CHUNKS):
         gather(I_Y, k).wait_recv()
         gather(I_FWD, k).start()
         gather(T_Y, k).wait_recv()
-        gather(T_FWD, k).start()
+        if k < CHUNKS - ACROSS:
+            gather(T_FWD, k).start()
+        else:
+
+            @pl.when(odd == 0)
+            def _():
+                gather(T_FWD, k).start()
+
         if k == CHUNKS - 2:
             for j in range(CHUNKS):
                 gather(I_CORE, j).wait_recv()

time: 43.9 us -> 43.9 us (level)
  the two profiles are of different devices: /device:TPU:141 before, /device:TPU:9 now
where the time goes in v5:
time: 43.9 us; the launch traced here: 43.7 us
  Pallas kernels  41.8 us (95%)
  between operations  1.93 us (4%)
    pallas_call x1, Pallas kernels, per_device(): pl.pallas_call(functools.partial(kernel, quarter, rows), out_shape=(pltpu...  40.9 us

profile of v5, /device:TPU:9, one launch (start us, length us, event | category | flops | bytes accessed | tf_op | source)
XLA Modules:
  0.0 43.7 jit_solution(4127409800388299217)
XLA Ops:
  1.9 40.9 %contrastive.1 = (bf16[128,1152]{1,0:T(8,128)(2,1)S(1)}, bf16[128,1152]{1,0:T(8,128)(2,1)S(1)}) custom-call(f32[1]{0:T(128)S(6)} %copy.6.scale_ref, f32[1]{0:T(128)S(6)} %copy.7.bias_ref, bf16[128,1152]{1,0:T(8,128)(2,1)} %image_ref.1, bf16[128,1152]{1,0:T(8,128)(2,1)} %text_ref.1), custom_call_target="tpu_custom_call" | custom-call | flops 1811939328 | bytes 1179648 | tf_op jit(solution)/shard_map/contrastive/pallas_call | solution.py:267
  42.9 0.8 %write_out.1 = (bf16[128,1152]{1,0:T(8,128)(2,1)}, bf16[128,1152]{1,0:T(8,128)(2,1)}) custom-call(bf16[128,1152]{1,0:T(8,128)(2,1)S(1)} %get-tuple-element.4.image_ref, bf16[128,1152]{1,0:T(8,128)(2,1)S(1)} %get-tuple-element.5.text_ref), custom_call_target="tpu_custom_call" | custom-call | tf_op jit(solution)/shard_map/write_out/pallas_call | solution.py:295

commit v6 on v4

--- a/solution.py
+++ b/solution.py
@@ -115,8 +115,8 @@
     @pl.when(odd == 0)
     def _():
         for k in range(CHUNKS):
+            gather(T_Y, k).start()
             gather(I_Y, k).start()
-            gather(T_Y, k).start()
 
     for k in range(CHUNKS):
         gather(T_Z, k).start()
@@ -127,13 +127,13 @@
         for k in range(LEAD):
             gather(T_Z, k).wait_recv()
         for k in range(CHUNKS):
+            gather(T_Y, k).start()
             gather(I_Y, k).start()
-            gather(T_Y, k).start()
-    for k in range(CHUNKS):
+    for k in range(CHUNKS):
+        gather(T_Y, k).wait_recv()
+        gather(T_FWD, k).start()
         gather(I_Y, k).wait_recv()
         gather(I_FWD, k).start()
-        gather(T_Y, k).wait_recv()
-        gather(T_FWD, k).start()
         if k == CHUNKS - 2:
             for j in range(CHUNKS):
                 gather(I_CORE, j).wait_recv()

time: 43.9 us -> 44 us (level)
  the two profiles are of different devices: /device:TPU:141 before, /device:TPU:8 now
where the time goes in v6:
time: 44 us; the launch traced here: 43.9 us
  Pallas kernels  41.9 us (95%)
  between operations  1.93 us (4%)
    pallas_call x1, Pallas kernels, per_device(): pl.pallas_call(functools.partial(kernel, quarter, rows), out_shape=(pltpu...  41.1 us

profile of v6, /device:TPU:8, one launch (start us, length us, event | category | flops | bytes accessed | tf_op | source)
XLA Modules:
  0.0 43.9 jit_solution(1304932456636235885)
XLA Ops:
  1.9 41.1 %contrastive.1 = (bf16[128,1152]{1,0:T(8,128)(2,1)S(1)}, bf16[128,1152]{1,0:T(8,128)(2,1)S(1)}) custom-call(f32[1]{0:T(128)S(6)} %copy.6.scale_ref, f32[1]{0:T(128)S(6)} %copy.7.bias_ref, bf16[128,1152]{1,0:T(8,128)(2,1)} %image_ref.1, bf16[128,1152]{1,0:T(8,128)(2,1)} %text_ref.1), custom_call_target="tpu_custom_call" | custom-call | flops 1811939328 | bytes 1179648 | tf_op jit(solution)/shard_map/contrastive/pallas_call | solution.py:247
  43.0 0.8 %write_out.1 = (bf16[128,1152]{1,0:T(8,128)(2,1)}, bf16[128,1152]{1,0:T(8,128)(2,1)}) custom-call(bf16[128,1152]{1,0:T(8,128)(2,1)S(1)} %get-tuple-element.4.image_ref, bf16[128,1152]{1,0:T(8,128)(2,1)S(1)} %get-tuple-element.5.text_ref), custom_call_target="tpu_custom_call" | custom-call | tf_op jit(solution)/shard_map/write_out/pallas_call | solution.py:275

commit v7 on v4

--- a/solution.py
+++ b/solution.py
@@ -11,7 +11,7 @@
 CHUNKS = 4
 LEAD = 4
 EARLY = 2
-AHEAD = 2
+AHEAD = 3
 F32 = jnp.float32
 BF16 = jnp.bfloat16
 

time: 43.9 us -> 43.9 us (level)
  no operation moved by 1% of the time
where the time goes in v7:
time: 43.9 us; the launch traced here: 43.7 us
  Pallas kernels  41.8 us (95%)
  between operations  1.93 us (4%)
    pallas_call x1, Pallas kernels, per_device(): pl.pallas_call(functools.partial(kernel, quarter, rows), out_shape=(pltpu...  41 us

profile of v7, /device:TPU:141, one launch (start us, length us, event | category | flops | bytes accessed | tf_op | source)
XLA Modules:
  0.0 43.7 jit_solution(4167499489560616005)
XLA Ops:
  1.9 41.0 %contrastive.1 = (bf16[128,1152]{1,0:T(8,128)(2,1)S(1)}, bf16[128,1152]{1,0:T(8,128)(2,1)S(1)}) custom-call(f32[1]{0:T(128)S(6)} %copy.6.scale_ref, f32[1]{0:T(128)S(6)} %copy.7.bias_ref, bf16[128,1152]{1,0:T(8,128)(2,1)} %image_ref.1, bf16[128,1152]{1,0:T(8,128)(2,1)} %text_ref.1), custom_call_target="tpu_custom_call" | custom-call | flops 1811939328 | bytes 1179648 | tf_op jit(solution)/shard_map/contrastive/pallas_call | solution.py:247
  42.9 0.8 %write_out.1 = (bf16[128,1152]{1,0:T(8,128)(2,1)}, bf16[128,1152]{1,0:T(8,128)(2,1)}) custom-call(bf16[128,1152]{1,0:T(8,128)(2,1)S(1)} %get-tuple-element.4.image_ref, bf16[128,1152]{1,0:T(8,128)(2,1)S(1)} %get-tuple-element.5.text_ref), custom_call_target="tpu_custom_call" | custom-call | tf_op jit(solution)/shard_map/write_out/pallas_call | solution.py:275
